TPU v7x, 256 devices: a whole 4x4x8 slice. The times are simulated.
256 devices in a mesh: batch: 16 (over z, core), proto: 16 (over y, x).
Axes of the slice: x: 4, y: 4, z: 8, core: 2. Of those that a mesh axis runs over, the one named last changes fastest.
Arguments:
- student_features: bfloat16 [10, 2048, 256], P(None, 'batch'), may hold values from -8 to 8
- teacher_features: bfloat16 [2, 2048, 256], P(None, 'batch'), may hold values from -8 to 8
- student_prototypes: bfloat16 [256, 65536], P(None, 'proto'), may hold values from -0.5 to 0.5
- teacher_prototypes: bfloat16 [256, 65536], P(None, 'proto'), may hold values from -0.5 to 0.5
Outputs:
- mean_loss: float32 [], replicated
- grad_features: float32 [10, 2048, 256], P(None, ('batch', 'proto'))
- grad_prototypes: float32 [256, 65536], P('batch', 'proto')
All inputs are finite; a program needn't handle non-finite values.
Results may differ from a plain program's by a relative error of at most 0.001.
The roundings to bfloat16 on the way count: a program that leaves them out, or rounds other values in their place, can miss the bound.
Values sent between devices are 32-bit elements; how exact they have to be, the bound alone decides.
A program may use at most 192 MiB of HBM per device.

v0:
```python
import jax
import jax.numpy as jnp
from jax import lax
from jax.sharding import PartitionSpec as P

CLUSTER_NUMBER = 65536
WIDE_CROP_NUMBER = 2
SK_ITERS = 3
PAIRS = 18
STUDENT_TEMP = 0.1
TEACHER_TEMP = 0.07
NORM_EPS = 1e-06


def unit_rows(values):
    floats = values.astype(jnp.float32)
    inverse = lax.rsqrt(jnp.sum(floats * floats, axis=-1, keepdims=True) + NORM_EPS)
    return (floats * inverse, inverse)


def unit_columns(values):
    floats = values.astype(jnp.float32)
    inverse = lax.rsqrt(jnp.sum(floats * floats, axis=0, keepdims=True) + NORM_EPS)
    return (floats * inverse, inverse)


def proto_step(cluster_share):
    column_mass = lax.psum(jnp.sum(cluster_share, axis=0), "batch")
    return cluster_share / (CLUSTER_NUMBER * column_mass[None, :])


def full_sweep(cluster_share, sample_number):
    cluster_share = proto_step(cluster_share)
    row_mass = lax.psum(jnp.sum(cluster_share, axis=1), "proto")
    return cluster_share / (sample_number * row_mass[:, None])


def on_device(student_features, teacher_features, student_prototypes, teacher_prototypes):
    crop_count, img_local, feature_dim = student_features.shape
    proto_local = student_prototypes.shape[1]
    batch_devices = lax.axis_size("batch")
    proto_devices = lax.axis_size("proto")
    images_all = img_local * batch_devices
    teacher_rows = WIDE_CROP_NUMBER * images_all
    student_count = crop_count * img_local
    unit_student, student_scale = unit_rows(student_features)
    student_bf = unit_student.astype(jnp.bfloat16).reshape(student_count, feature_dim)
    unit_proto, proto_scale = unit_columns(student_prototypes)
    proto_bf = unit_proto.astype(jnp.bfloat16)
    unit_teacher, unused_scale = unit_rows(teacher_features)
    teacher_bf = unit_teacher.astype(jnp.bfloat16).reshape(
        WIDE_CROP_NUMBER * img_local, feature_dim
    )
    unit_tproto, unused_tscale = unit_columns(teacher_prototypes)
    teacher_proto_bf = unit_tproto.astype(jnp.bfloat16)
    cluster_share = jnp.exp(
        jnp.dot(teacher_bf, teacher_proto_bf, preferred_element_type=jnp.float32) / TEACHER_TEMP
    )
    logits = jnp.dot(student_bf, proto_bf, preferred_element_type=jnp.float32) / STUDENT_TEMP
    exp_partial = jnp.sum(jnp.exp(logits), axis=1)
    for sweep_index in range(SK_ITERS):
        cluster_share = full_sweep(cluster_share, teacher_rows)
    exp_total = lax.psum(exp_partial, "proto")
    cluster_targets_matrix = (teacher_rows * cluster_share).reshape(
        WIDE_CROP_NUMBER, img_local, proto_local
    )
    first_global = cluster_targets_matrix[0]
    second_global = cluster_targets_matrix[1]
    summed = first_global + second_global
    targets = jnp.concatenate(
        [
            second_global[None],
            first_global[None],
            jnp.broadcast_to(summed[None], (crop_count - 2, img_local, proto_local)),
        ],
        axis=0,
    )
    pair_count = jnp.where(jnp.arange(crop_count) < 2, jnp.float32(1.0), jnp.float32(2.0))[
        :, None, None
    ]
    log_norm = jnp.log(exp_total).reshape(crop_count, img_local, 1)
    logits_crop = logits.reshape(crop_count, img_local, proto_local)
    loss_part = jnp.sum(targets * (log_norm - logits_crop))
    mean_loss = lax.psum(loss_part, ("batch", "proto")) / (images_all * PAIRS)
    factor = 1.0 / (images_all * PAIRS * STUDENT_TEMP)
    grad_cos = ((pair_count * jnp.exp(logits_crop - log_norm) - targets) * factor).astype(
        jnp.bfloat16
    )
    grad_cos = grad_cos.reshape(student_count, proto_local)
    feature_cot = lax.dot_general(
        grad_cos, proto_bf, (((1,), (1,)), ((), ())), preferred_element_type=jnp.float32
    )
    feature_cot = feature_cot.reshape(crop_count, img_local, feature_dim)
    own_count = img_local // proto_devices
    own_start = lax.axis_index("proto") * own_count
    cot_total = lax.psum(feature_cot, "proto")
    cot_own = lax.dynamic_slice_in_dim(cot_total, own_start, own_count, 1)
    unit_own = lax.dynamic_slice_in_dim(unit_student, own_start, own_count, 1)
    scale_own = lax.dynamic_slice_in_dim(student_scale, own_start, own_count, 1)
    grad_features = scale_own * (
        cot_own - unit_own * jnp.sum(unit_own * cot_own, axis=-1, keepdims=True)
    )
    curvature = jnp.sum(logits * STUDENT_TEMP * grad_cos.astype(jnp.float32), axis=0)
    rows_here = feature_dim // batch_devices
    product = lax.dot_general(
        student_bf, grad_cos, (((0,), (0,)), ((), ())), preferred_element_type=jnp.float32
    )
    term_total = lax.psum(product - unit_proto * curvature[None, :], "batch")
    term_own = lax.dynamic_slice_in_dim(
        term_total, lax.axis_index("batch") * rows_here, rows_here, 0
    )
    grad_prototypes = proto_scale * term_own
    return (mean_loss, grad_features, grad_prototypes)


def solution(mesh):
    placed = (P(None, "batch", None), P(None, "batch", None), P(None, "proto"), P(None, "proto"))
    return jax.shard_map(
        on_device,
        mesh=mesh,
        in_specs=placed,
        out_specs=(P(), P(None, ("batch", "proto"), None), P("batch", "proto")),
        check_vma=False,
    )
```

profile of v0, /device:TPU:1, one launch (start us, length us, event | category | flops | bytes accessed | tf_op | source)
XLA Modules:
  0.0 586.5 jit_solution(13375280952865046598)
XLA Ops:
  9.3 2.0 fusion.16
  11.3 4.6 fusion.46
  16.0 48.8 %psum.70 = f32[4096]{0:T(1024)S(1)} all-reduce(f32[4096]{0:T(1024)S(1)} %get-tuple-element.17), channel_id=1, replica_groups=mesh['batch'=16,'proto'=16] {'batch'}, use_global_device_ids=true, to_apply=%region_3.0 | all-reduce | flops 4096 | bytes 32768 | tf_op jit(solution)/shard_map/psum | solution.py:28
  64.8 2.6 divide_reduce_fusion
  67.3 33.6 %psum.71 = f32[256]{0:T(256)S(1)} all-reduce(f32[256]{0:T(256)S(1)} %divide_reduce_fusion), channel_id=1, replica_groups=mesh['batch'=16,'proto'=16] {'proto'}, use_global_device_ids=true, to_apply=%region_5.0 | all-reduce | flops 256 | bytes 2048 | tf_op jit(solution)/shard_map/psum | solution.py:34
  100.9 3.0 fusion.21
  103.9 52.8 %psum.72 = f32[4096]{0:T(1024)S(1)} all-reduce(f32[4096]{0:T(1024)S(1)} %fusion.21), channel_id=1, replica_groups=mesh['batch'=16,'proto'=16] {'batch'}, use_global_device_ids=true, to_apply=%region_7.0 | all-reduce | flops 4096 | bytes 32768 | tf_op jit(solution)/shard_map/psum | solution.py:28
  156.7 3.0 fusion.22
  159.7 28.5 %psum.73 = f32[256]{0:T(256)S(1)} all-reduce(f32[256]{0:T(256)S(1)} %fusion.22), channel_id=1, replica_groups=mesh['batch'=16,'proto'=16] {'proto'}, use_global_device_ids=true, to_apply=%region_9.0 | all-reduce | flops 256 | bytes 2048 | tf_op jit(solution)/shard_map/psum | solution.py:34
  188.2 3.2 fusion.23
  191.5 52.8 %psum.74 = f32[4096]{0:T(1024)S(1)} all-reduce(f32[4096]{0:T(1024)S(1)} %fusion.23), channel_id=1, replica_groups=mesh['batch'=16,'proto'=16] {'batch'}, use_global_device_ids=true, to_apply=%region_11.0 | all-reduce | flops 4096 | bytes 32768 | tf_op jit(solution)/shard_map/psum | solution.py:28
  244.3 3.4 fusion.24
  249.7 15.4 %broadcast_multiply_fusion = (f32[1280,4096]{1,0:T(8,128)}, f32[1280]{0:T(1024)S(1)}, f32[1280,4096]{1,0:T(8,128)}) fusion(bf16[1280,256]{1,0:T(8,128)(2,1)S(1)} %bitcast.37, bf16[256,4096]{1,0:T(8,128)(2,1)S(1)} %copy-done.1, f32[4096]{0:T(1024)S(1)} %add_rsqrt_fusion), kind=kOutput, calls=%fused_computation.10 | convolution fusion | flops 2697984768 | bytes 44717056 | tf_op jit(solution)/shard_map/dot_general | solution.py:59
  265.1 31.4 %all-reduce = (f32[256]{0:T(256)S(1)}, f32[1280]{0:T(1024)S(1)}) all-reduce(f32[256]{0:T(256)S(1)} %fusion.24, f32[1280]{0:T(1024)S(1)} %get-tuple-element.9), channel_id=1, replica_groups=mesh['batch'=16,'proto'=16] {'proto'}, use_global_device_ids=true, to_apply=%region_13.0 | all-reduce | flops 1536 | bytes 12288 | tf_op jit(solution)/shard_map/psum | solution.py:34
  296.5 3.5 fusion.20
  300.8 7.8 %broadcast_in_dim.8 = f32[8,128,4096]{2,1,0:T(8,128)} broadcast(f32[128,4096]{1,0:T(8,128)S(1)} %get-tuple-element.11), dimensions={1,2} | broadcast | bytes 18874368 | tf_op jit(solution)/shard_map/broadcast_in_dim | solution.py:74
  308.7 16.9 %pad_maximum_fusion = f32[10,128,4096]{2,1,0:T(8,128)} fusion(f32[8,128,4096]{2,1,0:T(8,128)} %broadcast_in_dim.8, f32[1,128,4096]{2,1,0:T(8,128)S(1)} %get-tuple-element.12, f32[1,128,4096]{2,1,0:T(8,128)S(1)} %get-tuple-element.10), kind=kLoop, calls=%fused_computation.1 | loop fusion | flops 10485760 | bytes 41943040 | tf_op jit(solution)/shard_map/concatenate | solution.py:70
  328.2 16.6 %multiply_reduce_fusion = (f32[4096]{0:T(1024)S(1)}, f32[]{:T(128)}, bf16[1280,4096]{1,0:T(8,128)(2,1)}) fusion(f32[1280,4096]{1,0:T(8,128)S(1)} %bitcast.34, f32[1280]{0:T(1024)S(1)} %get-tuple-element.16, f32[10,128,4096]{2,1,0:T(8,128)} %pad_maximum_fusion, f32[1280]{0:T(1024)S(1)} %broadcast_bitcast_fusion), kind=kLoop, calls=%fused_computation.7 | loop fusion | flops 62910464 | bytes 52455428 | tf_op jit(solution)/shard_map/reduce_sum | solution.py:103
  344.8 8.0 %fusion.26 = f32[10,128,256]{2,1,0:T(8,128)} fusion(bf16[10,128,4096]{2,1,0:T(8,128)(2,1)} %bitcast.36, bf16[256,4096]{1,0:T(8,128)(2,1)S(1)} %copy-done.2, f32[4096]{0:T(1024)S(1)} %add_rsqrt_fusion), kind=kOutput, calls=%fused_computation.40 | convolution fusion | flops 2687500288 | bytes 13910016 | tf_op jit(solution)/shard_map/dot_general | solution.py:90
  352.9 17.9 %fusion.13 = f32[256,4096]{1,0:T(8,128)} fusion(bf16[10,128,256]{2,1,0:T(8,128)(2,1)S(1)} %get-tuple-element.14, f32[10,128,4096]{2,1,0:T(8,128)} %bitcast.35, f32[10,128]{1,0:T(8,128)S(1)} %get-tuple-element.15, f32[10]{0:T(128)S(1)} %compare_select_fusion, bf16[256,4096]{1,0:T(8,128)(2,1)} %param.6, f32[8,128,4096]{2,1,0:T(8,128)} %broadcast_in_dim.8, ...), kind=kOutput, calls=%fused_computation.27 | convolution fusion | flops 2725249024 | bytes 48927784 | tf_op jit(solution)/shard_map/dot_general | solution.py:105
  370.8 82.0 %psum.77 = f32[]{:T(128)} all-reduce(f32[]{:T(128)} %get-tuple-element.4), channel_id=1, replica_groups=mesh['batch'=16,'proto'=16] {'batch','proto'}, use_global_device_ids=true, to_apply=%region_19.20 | all-reduce | flops 1 | bytes 8 | tf_op jit(solution)/shard_map/psum | solution.py:84
  453.5 1.8 fusion.35
  455.3 121.5 %all-reduce.6.cloned.1.call-done = f32[256,4096]{1,0:T(8,128)} async-done(((f32[256,4096]{1,0:T(8,128)}), f32[256,4096]{1,0:T(8,128)}) %all-reduce.6.cloned.1.call-update) | async-done | bytes 4194320 | tf_op jit(solution)/shard_map/psum | solution.py:108
  576.8 1.7 dynamic-slice_multiply_fusion
  (44 shorter events, 7.7 us)
Async XLA Ops:
  7.2 446.3 %all-reduce.4.cloned.1.call-start = ((), (), s32[]{:S(2)}) async-start(), calls=%async_computation | async-start | bytes 2621440 | tf_op jit(solution)/shard_map/psum | solution.py:96
  188.2 59.4 %copy-start.3 = (bf16[10,128,256]{2,1,0:T(8,128)(2,1)S(1)}, bf16[10,128,256]{2,1,0:T(8,128)(2,1)}, u32[]{:S(2)}) copy-start(bf16[10,128,256]{2,1,0:T(8,128)(2,1)} %param.4) | copy-start | bytes 1966084
  191.5 57.7 %copy-start.1 = (bf16[256,4096]{1,0:T(8,128)(2,1)S(1)}, bf16[256,4096]{1,0:T(8,128)(2,1)}, u32[]{:S(2)}) copy-start(bf16[256,4096]{1,0:T(8,128)(2,1)} %param.6) | copy-start | bytes 6291460
  300.7 7.9 %copy-start = (f32[1,128,4096]{2,1,0:T(8,128)}, f32[1,128,4096]{2,1,0:T(8,128)S(1)}, u32[]{:S(2)}) copy-start(f32[1,128,4096]{2,1,0:T(8,128)S(1)} %get-tuple-element.12) | copy-start | bytes 6291460
  308.6 17.0 %slice-start = ((s8[20971520]{0:T(1024)(128)(4,1)}), s8[4194304]{0:T(1024)(128)(4,1)S(1)}, s32[]{:S(2)}) async-start(s8[20971520]{0:T(1024)(128)(4,1)} %bitcast.33), calls=%async_computation.2 | async-start | bytes 8388608
  308.6 17.0 %slice-start.1 = ((s8[20971520]{0:T(1024)(128)(4,1)}), s8[4194304]{0:T(1024)(128)(4,1)S(1)}, s32[]{:S(2)}) async-start(s8[20971520]{0:T(1024)(128)(4,1)} %bitcast.33), calls=%async_computation.3 | async-start | bytes 8388608
  308.6 17.0 %slice-start.2 = ((s8[20971520]{0:T(1024)(128)(4,1)}), s8[4194304]{0:T(1024)(128)(4,1)S(1)}, s32[]{:S(2)}) async-start(s8[20971520]{0:T(1024)(128)(4,1)} %bitcast.33), calls=%async_computation.4 | async-start | bytes 8388608
  308.6 18.4 %slice-start.3 = ((s8[20971520]{0:T(1024)(128)(4,1)}), s8[4194304]{0:T(1024)(128)(4,1)S(1)}, s32[]{:S(2)}) async-start(s8[20971520]{0:T(1024)(128)(4,1)} %bitcast.33), calls=%async_computation.5 | async-start | bytes 8388608
  308.6 19.6 %slice-start.4 = ((s8[20971520]{0:T(1024)(128)(4,1)}), s8[4194304]{0:T(1024)(128)(4,1)S(1)}, s32[]{:S(2)}) async-start(s8[20971520]{0:T(1024)(128)(4,1)} %bitcast.33), calls=%async_computation.6 | async-start | bytes 8388608
  328.2 16.6 %copy-start.2 = (bf16[256,4096]{1,0:T(8,128)(2,1)S(1)}, bf16[256,4096]{1,0:T(8,128)(2,1)}, u32[]{:S(2)}) copy-start(bf16[256,4096]{1,0:T(8,128)(2,1)} %param.6) | copy-start | bytes 6291460
  352.8 224.0 %all-reduce.6.cloned.1.call-start = ((), (), s32[]{:S(2)}) async-start(), calls=%async_computation.1 | async-start | bytes 8388608 | tf_op jit(solution)/shard_map/psum | solution.py:108
Sparse Core Ops, SparseCore 0:
  352.9 99.8 all-reduce.3
  455.2 121.5 all-reduce.5
where the time goes:
time: 587 us; the launch traced here: 586 us
  blocking collectives  330 us (56%)
  waiting for transfers between devices  122 us (21%)
  other arithmetic  62.5 us (11%)
  matrix products  45.9 us (8%)
  between operations  16 us (3%)
  local copies, waits for them, and re-layouts  10.6 us (2%)
    psum x3, blocking collectives, proto_step(): column_mass = lax.psum(jnp.sum(cluster_share, axis=0), 'batch')  154 us
    psum x1, waiting for transfers between devices, on_device(): term_total = lax.psum(product - unit_proto * curvature[None, :], 'batch')  121 us
    psum x3, blocking collectives, full_sweep(): row_mass = lax.psum(jnp.sum(cluster_share, axis=1), 'proto')  93.5 us
    psum x1, blocking collectives, on_device(): mean_loss = lax.psum(loss_part, ('batch', 'proto')) / (images_all * PAIRS)  82 us
    dot_general x1, matrix products, on_device(): lax.dot_general(student_bf, grad_cos, (((0,), (0,)), ((), ())), preferred...  17.9 us
    concatenate x1, other arithmetic, on_device(): jnp.concatenate([second_global[None], first_global[None], jnp.broadcast_t...  16.9 us
    reduce_sum x1, other arithmetic, on_device(): jnp.sum(logits * STUDENT_TEMP * grad_cos.astype(jnp.float32), axis=0)  16.6 us
    dot_general x1, matrix products, on_device(): jnp.dot(student_bf, proto_bf, preferred_element_type=jnp.float32)  15.4 us
  transfers between devices with their start and end apart: 2, of which 1 were waited for; matrix products, arithmetic and copies ran while one was open for 3% of the time, Pallas kernels for 0%

commit v1 on v0

--- a/solution.py
+++ b/solution.py
@@ -25,7 +25,7 @@
 
 
 def proto_step(cluster_share):
-    column_mass = lax.psum(jnp.sum(cluster_share, axis=0), "batch")
+    column_mass = jnp.sum(lax.all_gather(jnp.sum(cluster_share, axis=0), "batch"), axis=0)
     return cluster_share / (CLUSTER_NUMBER * column_mass[None, :])
 
 

time: 587 us -> 498 us (0.85)
  blocking collectives: 330 us -> 240 us
    psum x3 -> x0, blocking collectives: 154 us -> none  [proto_step(): column_mass = lax.psum(jnp.sum(cluster_share, axis=0), 'batch')]
    all_gather x0 -> x3, blocking collectives: none -> 67.8 us  [proto_step(): lax.all_gather(jnp.sum(cluster_share, axis=0), 'batch')]
  transfers between devices with their start and end apart: 2 -> 2, of which waited for: 1 -> 1; matrix products, arithmetic and copies ran while one was open for 3% -> 4% of each run, Pallas kernels for 0% -> 0%
where the time goes in v1:
time: 498 us; the launch traced here: 497 us
  blocking collectives  240 us (48%)
  waiting for transfers between devices  121 us (24%)
  other arithmetic  62.7 us (13%)
  matrix products  46.2 us (9%)
  between operations  16 us (3%)
  local copies, waits for them, and re-layouts  10.8 us (2%)
    psum x1, waiting for transfers between devices, on_device(): term_total = lax.psum(product - unit_proto * curvature[None, :], 'batch')  121 us
    psum x3, blocking collectives, full_sweep(): row_mass = lax.psum(jnp.sum(cluster_share, axis=1), 'proto')  93.3 us
    psum x1, blocking collectives, on_device(): mean_loss = lax.psum(loss_part, ('batch', 'proto')) / (images_all * PAIRS)  78.4 us
    all_gather x3, blocking collectives, proto_step(): lax.all_gather(jnp.sum(cluster_share, axis=0), 'batch')  67.8 us
    dot_general x1, matrix products, on_device(): lax.dot_general(student_bf, grad_cos, (((0,), (0,)), ((), ())), preferred...  18.1 us
    concatenate x1, other arithmetic, on_device(): jnp.concatenate([second_global[None], first_global[None], jnp.broadcast_t...  16.9 us
    reduce_sum x1, other arithmetic, on_device(): jnp.sum(logits * STUDENT_TEMP * grad_cos.astype(jnp.float32), axis=0)  16.6 us
    dot_general x1, matrix products, on_device(): jnp.dot(student_bf, proto_bf, preferred_element_type=jnp.float32)  15.4 us
  transfers between devices with their start and end apart: 2, of which 1 were waited for; matrix products, arithmetic and copies ran while one was open for 4% of the time, Pallas kernels for 0%

profile of v1, /device:TPU:1, one launch (start us, length us, event | category | flops | bytes accessed | tf_op | source)
XLA Modules:
  0.0 496.9 jit_solution(8580483979239849079)
XLA Ops:
  9.3 2.0 fusion.16
  11.3 4.6 fusion.46
  16.0 22.0 %all-gather = f32[65536]{0:T(1024)S(1)} all-gather(f32[4096]{0:T(1024)S(1)} %get-tuple-element.17), channel_id=2, replica_groups=mesh['batch'=16,'proto'=16] {'batch'}, dimensions={0}, use_global_device_ids=true | all-gather | bytes 278528 | tf_op jit(solution)/shard_map/all_gather | solution.py:28
  38.1 2.6 divide_reduce_fusion
  40.6 33.5 %psum.49 = f32[256]{0:T(256)S(1)} all-reduce(f32[256]{0:T(256)S(1)} %divide_reduce_fusion), channel_id=1, replica_groups=mesh['batch'=16,'proto'=16] {'proto'}, use_global_device_ids=true, to_apply=%region_5.0 | all-reduce | flops 256 | bytes 2048 | tf_op jit(solution)/shard_map/psum | solution.py:34
  74.1 3.0 fusion.21
  77.1 22.1 %all-gather.1 = f32[65536]{0:T(1024)S(1)} all-gather(f32[4096]{0:T(1024)S(1)} %fusion.21), channel_id=3, replica_groups=mesh['batch'=16,'proto'=16] {'batch'}, dimensions={0}, use_global_device_ids=true | all-gather | bytes 278528 | tf_op jit(solution)/shard_map/all_gather | solution.py:28
  99.3 3.0 fusion.22
  102.3 28.5 %psum.50 = f32[256]{0:T(256)S(1)} all-reduce(f32[256]{0:T(256)S(1)} %fusion.22), channel_id=1, replica_groups=mesh['batch'=16,'proto'=16] {'proto'}, use_global_device_ids=true, to_apply=%region_9.0 | all-reduce | flops 256 | bytes 2048 | tf_op jit(solution)/shard_map/psum | solution.py:34
  130.8 3.2 fusion.23
  134.1 23.8 %all-gather.2 = f32[65536]{0:T(1024)S(1)} all-gather(f32[4096]{0:T(1024)S(1)} %fusion.23), channel_id=4, replica_groups=mesh['batch'=16,'proto'=16] {'batch'}, dimensions={0}, use_global_device_ids=true | all-gather | bytes 278528 | tf_op jit(solution)/shard_map/all_gather | solution.py:28
  157.9 3.5 fusion.24
  163.5 15.4 %broadcast_multiply_fusion = (f32[1280,4096]{1,0:T(8,128)}, f32[1280]{0:T(1024)S(1)}, f32[1280,4096]{1,0:T(8,128)}) fusion(bf16[1280,256]{1,0:T(8,128)(2,1)S(1)} %bitcast.37, bf16[256,4096]{1,0:T(8,128)(2,1)S(1)} %copy-done.1, f32[4096]{0:T(1024)S(1)} %add_rsqrt_fusion), kind=kOutput, calls=%fused_computation.10 | convolution fusion | flops 2697984768 | bytes 44717056 | tf_op jit(solution)/shard_map/dot_general | solution.py:59
  178.9 31.4 %all-reduce = (f32[256]{0:T(256)S(1)}, f32[1280]{0:T(1024)S(1)}) all-reduce(f32[256]{0:T(256)S(1)} %fusion.24, f32[1280]{0:T(1024)S(1)} %get-tuple-element.9), channel_id=1, replica_groups=mesh['batch'=16,'proto'=16] {'proto'}, use_global_device_ids=true, to_apply=%region_13.0 | all-reduce | flops 1536 | bytes 12288 | tf_op jit(solution)/shard_map/psum | solution.py:34
  210.3 3.5 fusion.20
  214.6 7.8 %broadcast_in_dim.8 = f32[8,128,4096]{2,1,0:T(8,128)} broadcast(f32[128,4096]{1,0:T(8,128)S(1)} %get-tuple-element.11), dimensions={1,2} | broadcast | bytes 18874368 | tf_op jit(solution)/shard_map/broadcast_in_dim | solution.py:74
  222.5 16.9 %pad_maximum_fusion = f32[10,128,4096]{2,1,0:T(8,128)} fusion(f32[8,128,4096]{2,1,0:T(8,128)} %broadcast_in_dim.8, f32[1,128,4096]{2,1,0:T(8,128)S(1)} %get-tuple-element.12, f32[1,128,4096]{2,1,0:T(8,128)S(1)} %get-tuple-element.10), kind=kLoop, calls=%fused_computation.1 | loop fusion | flops 10485760 | bytes 41943040 | tf_op jit(solution)/shard_map/concatenate | solution.py:70
  242.0 16.6 %multiply_reduce_fusion = (f32[4096]{0:T(1024)S(1)}, f32[]{:T(128)}, bf16[1280,4096]{1,0:T(8,128)(2,1)}) fusion(f32[1280,4096]{1,0:T(8,128)S(1)} %bitcast.34, f32[1280]{0:T(1024)S(1)} %get-tuple-element.16, f32[10,128,4096]{2,1,0:T(8,128)} %pad_maximum_fusion, f32[1280]{0:T(1024)S(1)} %broadcast_bitcast_fusion), kind=kLoop, calls=%fused_computation.7 | loop fusion | flops 62910464 | bytes 52455428 | tf_op jit(solution)/shard_map/reduce_sum | solution.py:103
  258.6 8.0 %fusion.26 = f32[10,128,256]{2,1,0:T(8,128)} fusion(bf16[10,128,4096]{2,1,0:T(8,128)(2,1)} %bitcast.36, bf16[256,4096]{1,0:T(8,128)(2,1)S(1)} %copy-done.2, f32[4096]{0:T(1024)S(1)} %add_rsqrt_fusion), kind=kOutput, calls=%fused_computation.40 | convolution fusion | flops 2687500288 | bytes 13910016 | tf_op jit(solution)/shard_map/dot_general | solution.py:90
  266.7 18.1 %fusion.13 = f32[256,4096]{1,0:T(8,128)} fusion(bf16[10,128,256]{2,1,0:T(8,128)(2,1)S(1)} %get-tuple-element.14, f32[10,128,4096]{2,1,0:T(8,128)} %bitcast.35, f32[10,128]{1,0:T(8,128)S(1)} %get-tuple-element.15, f32[10]{0:T(128)S(1)} %compare_select_fusion, bf16[256,4096]{1,0:T(8,128)(2,1)} %param.6, f32[8,128,4096]{2,1,0:T(8,128)} %broadcast_in_dim.8, ...), kind=kOutput, calls=%fused_computation.27 | convolution fusion | flops 2725249024 | bytes 48927784 | tf_op jit(solution)/shard_map/dot_general | solution.py:105
  284.9 78.4 %psum.53 = f32[]{:T(128)} all-reduce(f32[]{:T(128)} %get-tuple-element.4), channel_id=1, replica_groups=mesh['batch'=16,'proto'=16] {'batch','proto'}, use_global_device_ids=true, to_apply=%region_19.20 | all-reduce | flops 1 | bytes 8 | tf_op jit(solution)/shard_map/psum | solution.py:84
  364.0 1.8 fusion.35
  365.8 121.5 %all-reduce.6.cloned.1.call-done = f32[256,4096]{1,0:T(8,128)} async-done(((f32[256,4096]{1,0:T(8,128)}), f32[256,4096]{1,0:T(8,128)}) %all-reduce.6.cloned.1.call-update) | async-done | bytes 4194320 | tf_op jit(solution)/shard_map/psum | solution.py:108
  487.3 1.7 dynamic-slice_multiply_fusion
  (50 shorter events, 8.0 us)
Async XLA Ops:
  7.2 356.9 %all-reduce.4.cloned.1.call-start = ((), (), s32[]{:S(2)}) async-start(), calls=%async_computation | async-start | bytes 2621440 | tf_op jit(solution)/shard_map/psum | solution.py:96
  130.8 30.6 %copy-start.3 = (bf16[10,128,256]{2,1,0:T(8,128)(2,1)S(1)}, bf16[10,128,256]{2,1,0:T(8,128)(2,1)}, u32[]{:S(2)}) copy-start(bf16[10,128,256]{2,1,0:T(8,128)(2,1)} %param.4) | copy-start | bytes 1966084
  157.8 5.2 %copy-start.1 = (bf16[256,4096]{1,0:T(8,128)(2,1)S(1)}, bf16[256,4096]{1,0:T(8,128)(2,1)}, u32[]{:S(2)}) copy-start(bf16[256,4096]{1,0:T(8,128)(2,1)} %param.6) | copy-start | bytes 6291460
  214.5 7.9 %copy-start = (f32[1,128,4096]{2,1,0:T(8,128)}, f32[1,128,4096]{2,1,0:T(8,128)S(1)}, u32[]{:S(2)}) copy-start(f32[1,128,4096]{2,1,0:T(8,128)S(1)} %get-tuple-element.12) | copy-start | bytes 6291460
  222.4 17.0 %slice-start = ((s8[20971520]{0:T(1024)(128)(4,1)}), s8[4194304]{0:T(1024)(128)(4,1)S(1)}, s32[]{:S(2)}) async-start(s8[20971520]{0:T(1024)(128)(4,1)} %bitcast.33), calls=%async_computation.2 | async-start | bytes 8388608
  222.4 17.0 %slice-start.1 = ((s8[20971520]{0:T(1024)(128)(4,1)}), s8[4194304]{0:T(1024)(128)(4,1)S(1)}, s32[]{:S(2)}) async-start(s8[20971520]{0:T(1024)(128)(4,1)} %bitcast.33), calls=%async_computation.3 | async-start | bytes 8388608
  222.4 17.0 %slice-start.2 = ((s8[20971520]{0:T(1024)(128)(4,1)}), s8[4194304]{0:T(1024)(128)(4,1)S(1)}, s32[]{:S(2)}) async-start(s8[20971520]{0:T(1024)(128)(4,1)} %bitcast.33), calls=%async_computation.4 | async-start | bytes 8388608
  222.5 18.4 %slice-start.3 = ((s8[20971520]{0:T(1024)(128)(4,1)}), s8[4194304]{0:T(1024)(128)(4,1)S(1)}, s32[]{:S(2)}) async-start(s8[20971520]{0:T(1024)(128)(4,1)} %bitcast.33), calls=%async_computation.5 | async-start | bytes 8388608
  222.5 19.6 %slice-start.4 = ((s8[20971520]{0:T(1024)(128)(4,1)}), s8[4194304]{0:T(1024)(128)(4,1)S(1)}, s32[]{:S(2)}) async-start(s8[20971520]{0:T(1024)(128)(4,1)} %bitcast.33), calls=%async_computation.6 | async-start | bytes 8388608
  242.0 16.6 %copy-start.2 = (bf16[256,4096]{1,0:T(8,128)(2,1)S(1)}, bf16[256,4096]{1,0:T(8,128)(2,1)}, u32[]{:S(2)}) copy-start(bf16[256,4096]{1,0:T(8,128)(2,1)} %param.6) | copy-start | bytes 6291460
  266.6 220.7 %all-reduce.6.cloned.1.call-start = ((), (), s32[]{:S(2)}) async-start(), calls=%async_computation.1 | async-start | bytes 8388608 | tf_op jit(solution)/shard_map/psum | solution.py:108
Sparse Core Ops, SparseCore 0:
  266.8 96.5 all-reduce.3
  365.7 121.5 all-reduce.5
